TPU v7x, 32 devices: a whole 2x2x4 slice. The times are simulated.
32 devices in a mesh: gz: 8 (over z, y), gy: 4 (over x, core).
Axes of the slice: x: 2, y: 2, z: 4, core: 2. Of those that a mesh axis runs over, the one named last changes fastest.
Arguments:
- concentration: float32 [128, 32, 128], P('gz', 'gy'), may hold values from 0 to 2
- phases: int32 [128, 32, 128], P('gz', 'gy'), may hold values from 0 to 2, as said below
- grains: int32 [128, 32, 128], P('gz', 'gy'), may hold values from 0 to 63, as said below
- grain_class: int32 [64], replicated, may hold values from 0 to 3
- diffusivity: float32 [3, 4], replicated, may hold values from 1 to 2000
Outputs:
- solution: float32 [128, 32, 128], P('gz', 'gy')
Inputs may be any that keep to these rules, and one draw needn't show every extreme that they name: `phases`: constant on aligned blocks of 8 x 8 x 8 cells. `grains`: constant on aligned blocks of 4 x 4 x 4 cells.
All inputs are finite; a program needn't handle non-finite values.
Results may differ from a plain program's by a relative error of at most 0.0003.
Values sent between devices are 32-bit elements; how exact they have to be, the bound alone decides.
A program may use at most 64 MiB of HBM per device.

v0:
```python
import jax
import jax.numpy as jnp
from jax import lax
from jax.sharding import PartitionSpec as P

CYCLES = 2
COARSE = 6


RELAX_WEIGHT = 0.8


def with_halo(array, sides, width):
    for axis, dim in sides:
        devices, length = (lax.axis_size(axis), array.shape[dim])
        up = [(i, (i + 1) % devices) for i in range(devices)]
        down = [(j, i) for i, j in up]
        last = lax.slice_in_dim(array, length - width, length, axis=dim)
        initial = lax.slice_in_dim(array, 0, width, axis=dim)
        before = lax.ppermute(last, axis, up)
        after = lax.ppermute(initial, axis, down)
        array = jnp.concatenate([before, array, after], axis=dim)
    return array


def harmonic(near_k, far_k):
    return 2.0 * near_k * far_k / (near_k + far_k)


def face_set(padded, margin, y_start, y_total):
    centre = padded[1:-1, 1:-1]
    row_index = lax.broadcasted_iota(jnp.int32, centre.shape, 1) + y_start - margin
    col_index = lax.broadcasted_iota(jnp.int32, centre.shape, 2)
    z_low = harmonic(centre, padded[:-2, 1:-1])
    z_high = harmonic(centre, padded[2:, 1:-1])
    y_low = jnp.where(row_index == 0, 0.0, harmonic(centre, padded[1:-1, :-2]))
    y_high = jnp.where(row_index == y_total - 1, 0.0, harmonic(centre, padded[1:-1, 2:]))
    x_low = jnp.where(col_index == 0, 0.0, harmonic(centre, jnp.roll(centre, 1, 2)))
    x_high = jnp.where(
        col_index == centre.shape[2] - 1, 0.0, harmonic(centre, jnp.roll(centre, -1, 2))
    )
    diagonal = 1.0 + z_low + z_high + y_low + y_high + x_low + x_high
    return (z_low, z_high, y_low, y_high, x_low, x_high, diagonal)


def cut_faces(faces, margin_cut):
    return tuple((face[margin_cut:-margin_cut, margin_cut:-margin_cut] for face in faces))


def apply_operator(padded, faces):
    z_low, z_high, y_low, y_high, x_low, x_high, diagonal = faces
    centre = padded[1:-1, 1:-1]
    coupled = (
        z_low * padded[:-2, 1:-1]
        + z_high * padded[2:, 1:-1]
        + y_low * padded[1:-1, :-2]
        + y_high * padded[1:-1, 2:]
        + x_low * jnp.roll(centre, 1, 2)
        + x_high * jnp.roll(centre, -1, 2)
    )
    return (centre, diagonal * centre - coupled)


def relax_sweep(padded, source, faces):
    centre, image = apply_operator(padded, faces)
    return centre + RELAX_WEIGHT * (source - image) / faces[6]


def defect(padded, source, faces):
    return source - apply_operator(padded, faces)[1]


def restrict(values):
    extent = values.shape
    return values.reshape(extent[0] // 2, 2, extent[1] // 2, 2, extent[2] // 2, 2).mean(
        axis=(1, 3, 5)
    )


def prolong(coarse):
    return jnp.repeat(jnp.repeat(jnp.repeat(coarse, 2, 0), 2, 1), 2, 2)


def pad_y_edge(values):
    return jnp.pad(values, ((0, 0), (1, 1), (0, 0)), mode="edge")


def cell_kappa(phases, grains, grain_class, diffusivity):
    num_grains = grain_class.shape[0]
    num_phases, num_classes = diffusivity.shape
    class_hot = (grain_class[:, None] == jnp.arange(num_classes, dtype=jnp.int32)[None, :]).astype(
        jnp.float32
    )
    by_grain = jnp.dot(class_hot, diffusivity.T, precision=lax.Precision.HIGHEST)
    entries = by_grain.T.reshape(-1)
    combined = phases * num_grains + grains
    labels = jnp.arange(num_phases * num_grains, dtype=jnp.int32)

    def one_plane(plane_ids):
        one_hot = (plane_ids[..., None] == labels).astype(jnp.float32)
        return jnp.dot(one_hot, entries, precision=lax.Precision.HIGHEST)

    return lax.map(one_plane, combined)


def split_faces(kappa):
    local_rows = kappa.shape[1]
    padded = with_halo(kappa, (("gz", 0), ("gy", 1)), 2)
    return face_set(padded, 1, lax.axis_index("gy") * local_rows, local_rows * lax.axis_size("gy"))


def whole_faces(kappa):
    padded = with_halo(kappa, (("gz", 0),), 1)
    return face_set(pad_y_edge(padded), 0, 0, kappa.shape[1])


def halo_split(field):
    return with_halo(field, (("gz", 0), ("gy", 1)), 1)


def halo_whole(field):
    return pad_y_edge(with_halo(field, (("gz", 0),), 1))


def smooth(field, source, faces, y_split):
    if y_split:
        inner_faces = cut_faces(faces, 1)
        for _ in range(2):
            field = relax_sweep(halo_split(field), source, inner_faces)
        return field
    for _ in range(2):
        field = relax_sweep(halo_whole(field), source, faces)
    return field


def coarsest(source, faces):
    field = jnp.zeros_like(source)
    for _ in range(COARSE):
        padded = pad_y_edge(with_halo(field, (("gz", 0),), 1))
        field = relax_sweep(padded, source, faces)
    return field


def descend(level_index, field, source, levels, coarse_all):
    faces, y_split = levels[level_index]
    if level_index == len(levels) - 1:
        return coarsest(source, faces)
    field = smooth(field, source, faces, y_split)
    if y_split:
        residual = defect(halo_split(field), source, cut_faces(faces, 1))
    else:
        residual = defect(halo_whole(field), source, faces)
    coarse_source = restrict(residual)
    local_rows = coarse_source.shape[1]
    if level_index == 1:
        coarse_source = lax.all_gather(coarse_source, "gy", axis=1, tiled=True)
    if level_index == 2:
        correction = descend(
            level_index + 1, jnp.zeros_like(coarse_source), coarse_source, levels, coarse_all
        )
    else:
        correction = descend(
            level_index + 1, jnp.zeros_like(coarse_source), coarse_source, levels, coarse_all
        )
    if level_index == 1:
        correction = lax.dynamic_slice_in_dim(
            correction, lax.axis_index("gy") * local_rows, local_rows, 1
        )
    field = field + prolong(correction)
    return smooth(field, source, faces, y_split)


def per_device(concentration, phases, grains, grain_class, diffusivity):
    kappa0 = cell_kappa(phases, grains, grain_class, diffusivity)
    kappa1 = 0.5 * restrict(kappa0)
    kappa2 = lax.all_gather(0.5 * restrict(kappa1), "gy", axis=1, tiled=True)
    kappa3 = 0.5 * restrict(kappa2)
    levels = [
        (split_faces(kappa0), True),
        (split_faces(kappa1), True),
        (whole_faces(kappa2), False),
    ]
    coarse_all = None
    kappa4 = 0.5 * restrict(kappa3)
    levels = levels + [(whole_faces(kappa3), False), (whole_faces(kappa4), False)]
    coarse_all = levels[4][0]
    field = jnp.zeros_like(concentration)
    for _ in range(CYCLES):
        field = descend(0, field, concentration, levels, coarse_all)
    return field


def solution(mesh):
    placed = (P("gz", "gy", None), P("gz", "gy", None), P("gz", "gy", None), P(), P())
    return jax.shard_map(
        per_device, mesh=mesh, in_specs=placed, out_specs=P("gz", "gy", None), check_vma=False
    )
```

profile of v0, /device:TPU:0, one launch (start us, length us, event | category | flops | bytes accessed | tf_op | source)
XLA Modules:
  0.0 462.4 jit_solution(8664263156337767632)
XLA Ops:
  0.0 3.0 collective-permute-start.4
  3.0 3.1 collective-permute-start.5
  10.0 10.5 %while.11 = (s32[]{:T(128)}, f32[16,8,128]{2,1,0:T(8,128)S(1)}, s32[16,8,128]{2,1,0:T(8,128)S(1)}, f32[192]{0:T(256)S(1)}, s32[]{:T(128)}) while((s32[]{:T(128)}, f32[16,8,128]{2,1,0:T(8,128)S(1)}, s32[16,8,128]{2,1,0:T(8,128)S(1)}, f32[192]{0:T(256)S(1)}, s32[]{:T(128)}) %tuple.242), condition=%wide.region_1.2_spmd.clone, body=%wide.region_0.1_spmd.clone.sunk | while | flops 2555906 | bytes 25421 | solution.py:103
  20.4 5.6 %reshape.2096 = f32[8,2,4,2,64,2]{5,4,3,2,1,0:T(8,128)} reshape(f32[16,8,128]{2,1,0:T(8,128)S(1)} %get-tuple-element.32) | data formatting | bytes 131072 | tf_op jit(solution)/shard_map/reshape | solution.py:75
  29.3 5.2 %all_gather.10 = f32[4,8,32]{2,0,1:T(4,128)S(1)} all-gather(f32[4,2,32]{2,0,1:T(4,128)S(1)} %broadcast_multiply_fusion.3), channel_id=1, replica_groups=mesh['gz'=8,'gy'=4] {'gy'}, dimensions={1}, use_global_device_ids=true | all-gather | bytes 5120 | tf_op jit(solution)/shard_map/all_gather | solution.py:176
  35.7 4.8 %collective-permute-start.49 = (f32[1,2,8]{2,1,0:T(2,128)S(1)}, f32[1,2,8]{2,1,0:T(2,128)S(1)}, u32[]{:S(2)}, u32[]{:S(2)}) collective-permute-start(f32[1,2,8]{2,1,0:T(2,128)S(1)} %multiply_bitcast_fusion), channel_id=1, source_target_pairs={{4,0},{8,4},{12,8},{16,12},{20,16},{24,20},{28,24},{0,28},{5,1},{9... | collective-permute-start | bytes 200 | tf_op jit(solution)/shard_map/ppermute | solution.py:21
  42.5 4.7 %collective-permute-start.21 = (f32[1,4,64]{2,1,0:T(4,128)S(1)}, f32[1,4,64]{2,1,0:T(4,128)S(1)}, u32[]{:S(2)}, u32[]{:S(2)}) collective-permute-start(f32[1,4,64]{2,1,0:T(4,128)S(1)} %broadcast.1095), channel_id=1, source_target_pairs={{4,0},{8,4},{12,8},{16,12},{20,16},{24,20},{28,24},{0,28},{5,1},{9... | collective-permute-start | bytes 3080 | tf_op jit(solution)/shard_map/ppermute | solution.py:21
  48.9 3.1 collective-permute-start.33
  53.7 4.7 %collective-permute-start.17 = (f32[2,4,64]{2,1,0:T(4,128)S(1)}, f32[2,4,64]{2,1,0:T(4,128)S(1)}, u32[]{:S(2)}, u32[]{:S(2)}) collective-permute-start(f32[2,4,64]{2,1,0:T(4,128)S(1)} %get-tuple-element.338), channel_id=1, source_target_pairs={{4,0},{8,4},{12,8},{16,12},{20,16},{24,20},{28,24},{0,28},{5,1},{9... | collective-permute-start | bytes 6152 | tf_op jit(solution)/shard_map/ppermute | solution.py:21
  60.0 3.3 collective-permute-start.43
  66.4 4.7 %collective-permute-start.1 = (f32[2,8,128]{2,1,0:T(8,128)S(1)}, f32[2,8,128]{2,1,0:T(8,128)S(1)}, u32[]{:S(2)}, u32[]{:S(2)}) collective-permute-start(f32[2,8,128]{2,1,0:T(8,128)S(1)} %get-tuple-element.259), channel_id=1, source_target_pairs={{4,0},{8,4},{12,8},{16,12},{20,16},{24,20},{28,24},{0,28},{5,1},{9... | collective-permute-start | bytes 24584 | tf_op jit(solution)/shard_map/ppermute | solution.py:21
  80.0 4.7 %collective-permute-start.9 = (f32[1,8,128]{2,1,0:T(8,128)S(1)}, f32[1,8,128]{2,1,0:T(8,128)S(1)}, u32[]{:S(2)}, u32[]{:S(2)}) collective-permute-start(f32[1,8,128]{2,1,0:T(8,128)S(1)} %get-tuple-element.258), channel_id=1, source_target_pairs={{4,0},{8,4},{12,8},{16,12},{20,16},{24,20},{28,24},{0,28},{5,1},{9... | collective-permute-start | bytes 12296 | tf_op jit(solution)/shard_map/ppermute | solution.py:21
  86.1 5.0 %collective-permute-done.8 = f32[1,8,128]{2,1,0:T(8,128)S(1)} collective-permute-done((f32[1,8,128]{2,1,0:T(8,128)S(1)}, f32[1,8,128]{2,1,0:T(8,128)S(1)}, u32[]{:S(2)}, u32[]{:S(2)}) %collective-permute-start.8) | collective-permute-done | bytes 4128 | tf_op jit(solution)/shard_map/ppermute | solution.py:20
  98.1 2.8 collective-permute-done.12
  104.4 5.6 %reshape.2095 = f32[8,2,4,2,64,2]{5,4,3,2,1,0:T(8,128)} reshape(f32[16,8,128]{2,1,0:T(8,128)S(1)} %fusion.233) | data formatting | bytes 131072 | tf_op jit(solution)/shard_map/reshape | solution.py:75
  116.3 2.8 collective-permute-done.24
  126.4 2.9 collective-permute-done.28
  133.3 5.4 %all_gather.9 = f32[4,8,32]{2,0,1:T(4,128)S(1)} all-gather(f32[4,2,32]{2,0,1:T(4,128)S(1)} %broadcast_multiply_fusion.5), channel_id=1, replica_groups=mesh['gz'=8,'gy'=4] {'gy'}, dimensions={1}, use_global_device_ids=true | all-gather | bytes 5120 | tf_op jit(solution)/shard_map/all_gather | solution.py:156
  142.8 2.8 collective-permute-done.36
  153.8 5.0 %collective-permute-start.45 = (f32[1,4,16]{2,1,0:T(4,128)S(1)}, f32[1,4,16]{2,1,0:T(4,128)S(1)}, u32[]{:S(2)}, u32[]{:S(2)}) collective-permute-start(f32[1,4,16]{2,1,0:T(4,128)S(1)} %get-tuple-element.384), channel_id=1, source_target_pairs={{4,0},{8,4},{12,8},{16,12},{20,16},{24,20},{28,24},{0,28},{5,1},{9... | collective-permute-start | bytes 776 | tf_op jit(solution)/shard_map/ppermute | solution.py:21
  160.1 5.0 %collective-permute-done.44 = f32[1,4,16]{2,1,0:T(4,128)S(1)} collective-permute-done((f32[1,4,16]{2,1,0:T(4,128)S(1)}, f32[1,4,16]{2,1,0:T(4,128)S(1)}, u32[]{:S(2)}, u32[]{:S(2)}) %collective-permute-start.44) | collective-permute-done | bytes 288 | tf_op jit(solution)/shard_map/ppermute | solution.py:20
  221.8 2.8 collective-permute-done.66
  301.0 5.6 %reshape.2109 = f32[8,2,4,2,64,2]{5,4,3,2,1,0:T(8,128)} reshape(f32[16,8,128]{2,1,0:T(8,128)S(1)} %fusion.107) | data formatting | bytes 131072 | tf_op jit(solution)/shard_map/reshape | solution.py:75
  329.5 5.2 %all_gather.11 = f32[4,8,32]{2,0,1:T(4,128)S(1)} all-gather(f32[4,2,32]{2,0,1:T(4,128)S(1)} %broadcast_multiply_fusion.4), channel_id=1, replica_groups=mesh['gz'=8,'gy'=4] {'gy'}, dimensions={1}, use_global_device_ids=true | all-gather | bytes 5120 | tf_op jit(solution)/shard_map/all_gather | solution.py:156
  (714 shorter events, 362.8 us)
Async XLA Ops:
  0.0 64.9 %collective-permute-start.4 = (f32[1,8,128]{2,1,0:T(8,128)S(1)}, f32[1,8,128]{2,1,0:T(8,128)S(1)}, u32[]{:S(2)}, u32[]{:S(2)}) collective-permute-start(f32[1,8,128]{2,1,0:T(8,128)S(1)} %broadcast.1087), channel_id=1, source_target_pairs={{0,4},{4,8},{8,12},{12,16},{16,20},{20,24},{24,28},{28,0},{1,5},{5... | collective-permute-start | bytes 12296 | tf_op jit(solution)/shard_map/ppermute | solution.py:20
  3.0 62.1 %collective-permute-start.5 = (f32[1,8,128]{2,1,0:T(8,128)S(1)}, f32[1,8,128]{2,1,0:T(8,128)S(1)}, u32[]{:S(2)}, u32[]{:S(2)}) collective-permute-start(f32[1,8,128]{2,1,0:T(8,128)S(1)} %broadcast.1087), channel_id=1, source_target_pairs={{4,0},{8,4},{12,8},{16,12},{20,16},{24,20},{28,24},{0,28},{5,1},{9... | collective-permute-start | bytes 12296 | tf_op jit(solution)/shard_map/ppermute | solution.py:21
  6.1 29.6 %collective-permute-start.51 = (f32[1,2,8]{2,1,0:T(2,128)S(1)}, f32[1,2,8]{2,1,0:T(2,128)S(1)}, u32[]{:S(2)}, u32[]{:S(2)}) collective-permute-start(f32[1,2,8]{2,1,0:T(2,128)S(1)} %slice.2445), channel_id=1, source_target_pairs={{4,0},{8,4},{12,8},{16,12},{20,16},{24,20},{28,24},{0,28},{5,1},{9... | collective-permute-start | bytes 200 | tf_op jit(solution)/shard_map/ppermute | solution.py:21
  8.0 32.4 %collective-permute-start.50 = (f32[1,2,8]{2,1,0:T(2,128)S(1)}, f32[1,2,8]{2,1,0:T(2,128)S(1)}, u32[]{:S(2)}, u32[]{:S(2)}) collective-permute-start(f32[1,2,8]{2,1,0:T(2,128)S(1)} %slice.2445), channel_id=1, source_target_pairs={{0,4},{4,8},{8,12},{12,16},{16,20},{20,24},{24,28},{28,0},{1,5},{5... | collective-permute-start | bytes 200 | tf_op jit(solution)/shard_map/ppermute | solution.py:20
  35.0 7.4 %collective-permute-start.48 = (f32[1,2,8]{2,1,0:T(2,128)S(1)}, f32[1,2,8]{2,1,0:T(2,128)S(1)}, u32[]{:S(2)}, u32[]{:S(2)}) collective-permute-start(f32[1,2,8]{2,1,0:T(2,128)S(1)} %multiply_bitcast_fusion), channel_id=1, source_target_pairs={{0,4},{4,8},{8,12},{12,16},{16,20},{20,24},{24,28},{28,0},{1,5},{5... | collective-permute-start | bytes 200 | tf_op jit(solution)/shard_map/ppermute | solution.py:20
  35.7 6.9 %collective-permute-start.49 = (f32[1,2,8]{2,1,0:T(2,128)S(1)}, f32[1,2,8]{2,1,0:T(2,128)S(1)}, u32[]{:S(2)}, u32[]{:S(2)}) collective-permute-start(f32[1,2,8]{2,1,0:T(2,128)S(1)} %multiply_bitcast_fusion), channel_id=1, source_target_pairs={{4,0},{8,4},{12,8},{16,12},{20,16},{24,20},{28,24},{0,28},{5,1},{9... | collective-permute-start | bytes 200 | tf_op jit(solution)/shard_map/ppermute | solution.py:21
  40.4 6.8 %collective-permute-start.35 = (f32[1,8,32]{1,2,0:T(8,128)S(1)}, f32[1,8,32]{1,2,0:T(8,128)S(1)}, u32[]{:S(2)}, u32[]{:S(2)}) collective-permute-start(f32[1,8,32]{1,2,0:T(8,128)S(1)} %broadcast.1101), channel_id=1, source_target_pairs={{4,0},{8,4},{12,8},{16,12},{20,16},{24,20},{28,24},{0,28},{5,1},{9... | collective-permute-start | bytes 3080 | tf_op jit(solution)/shard_map/ppermute | solution.py:21
  42.4 6.5 %collective-permute-start.34 = (f32[1,8,32]{1,2,0:T(8,128)S(1)}, f32[1,8,32]{1,2,0:T(8,128)S(1)}, u32[]{:S(2)}, u32[]{:S(2)}) collective-permute-start(f32[1,8,32]{1,2,0:T(8,128)S(1)} %broadcast.1101), channel_id=1, source_target_pairs={{0,4},{4,8},{8,12},{12,16},{16,20},{20,24},{24,28},{28,0},{1,5},{5... | collective-permute-start | bytes 3080 | tf_op jit(solution)/shard_map/ppermute | solution.py:20
  42.5 16.0 %collective-permute-start.21 = (f32[1,4,64]{2,1,0:T(4,128)S(1)}, f32[1,4,64]{2,1,0:T(4,128)S(1)}, u32[]{:S(2)}, u32[]{:S(2)}) collective-permute-start(f32[1,4,64]{2,1,0:T(4,128)S(1)} %broadcast.1095), channel_id=1, source_target_pairs={{4,0},{8,4},{12,8},{16,12},{20,16},{24,20},{28,24},{0,28},{5,1},{9... | collective-permute-start | bytes 3080 | tf_op jit(solution)/shard_map/ppermute | solution.py:21
  47.2 6.5 %collective-permute-start.32 = (f32[1,8,32]{1,2,0:T(8,128)S(1)}, f32[1,8,32]{1,2,0:T(8,128)S(1)}, u32[]{:S(2)}, u32[]{:S(2)}) collective-permute-start(f32[1,8,32]{1,2,0:T(8,128)S(1)} %get-tuple-element.246), channel_id=1, source_target_pairs={{0,4},{4,8},{8,12},{12,16},{16,20},{20,24},{24,28},{28,0},{1,5},{5... | collective-permute-start | bytes 3080 | tf_op jit(solution)/shard_map/ppermute | solution.py:20
  53.7 9.6 %collective-permute-start.17 = (f32[2,4,64]{2,1,0:T(4,128)S(1)}, f32[2,4,64]{2,1,0:T(4,128)S(1)}, u32[]{:S(2)}, u32[]{:S(2)}) collective-permute-start(f32[2,4,64]{2,1,0:T(4,128)S(1)} %get-tuple-element.338), channel_id=1, source_target_pairs={{4,0},{8,4},{12,8},{16,12},{20,16},{24,20},{28,24},{0,28},{5,1},{9... | collective-permute-start | bytes 6152 | tf_op jit(solution)/shard_map/ppermute | solution.py:21
  60.0 93.0 %collective-permute-start.43 = (f32[1,4,16]{2,1,0:T(4,128)S(1)}, f32[1,4,16]{2,1,0:T(4,128)S(1)}, u32[]{:S(2)}, u32[]{:S(2)}) collective-permute-start(f32[1,4,16]{2,1,0:T(4,128)S(1)} %broadcast.1106), channel_id=1, source_target_pairs={{4,0},{8,4},{12,8},{16,12},{20,16},{24,20},{28,24},{0,28},{5,1},{9... | collective-permute-start | bytes 776 | tf_op jit(solution)/shard_map/ppermute | solution.py:21
  63.4 89.7 %collective-permute-start.42 = (f32[1,4,16]{2,1,0:T(4,128)S(1)}, f32[1,4,16]{2,1,0:T(4,128)S(1)}, u32[]{:S(2)}, u32[]{:S(2)}) collective-permute-start(f32[1,4,16]{2,1,0:T(4,128)S(1)} %broadcast.1106), channel_id=1, source_target_pairs={{0,4},{4,8},{8,12},{12,16},{16,20},{20,24},{24,28},{28,0},{1,5},{5... | collective-permute-start | bytes 776 | tf_op jit(solution)/shard_map/ppermute | solution.py:20
  71.1 81.9 %collective-permute-start.40 = (f32[1,4,16]{2,1,0:T(4,128)S(1)}, f32[1,4,16]{2,1,0:T(4,128)S(1)}, u32[]{:S(2)}, u32[]{:S(2)}) collective-permute-start(f32[1,4,16]{2,1,0:T(4,128)S(1)} %get-tuple-element.394), channel_id=1, source_target_pairs={{0,4},{4,8},{8,12},{12,16},{16,20},{20,24},{24,28},{28,0},{1,5},{5... | collective-permute-start | bytes 776 | tf_op jit(solution)/shard_map/ppermute | solution.py:20
  102.4 10.2 %collective-permute-start.23 = (f32[10,1,64]{2,1,0:T(1,128)S(1)}, f32[10,1,64]{2,1,0:T(1,128)S(1)}, u32[]{:S(2)}, u32[]{:S(2)}) collective-permute-start(f32[10,1,64]{2,1,0:T(1,128)S(1)} %get-tuple-element.288), channel_id=1, source_target_pairs={{1,0},{2,1},{3,2},{0,3},{5,4},{6,5},{7,6},{4,7},{9,8},{10,9},{11,1... | collective-permute-start | bytes 7688 | tf_op jit(solution)/shard_map/ppermute | solution.py:21
  104.1 8.4 %collective-permute-start.22 = (f32[10,1,64]{2,1,0:T(1,128)S(1)}, f32[10,1,64]{2,1,0:T(1,128)S(1)}, u32[]{:S(2)}, u32[]{:S(2)}) collective-permute-start(f32[10,1,64]{2,1,0:T(1,128)S(1)} %get-tuple-element.287), channel_id=1, source_target_pairs={{0,1},{1,2},{2,3},{3,0},{4,5},{5,6},{6,7},{7,4},{8,9},{9,10},{10,1... | collective-permute-start | bytes 7688 | tf_op jit(solution)/shard_map/ppermute | solution.py:20
  139.1 6.5 %collective-permute-start.36 = (f32[1,8,32]{1,2,0:T(8,128)S(1)}, f32[1,8,32]{1,2,0:T(8,128)S(1)}, u32[]{:S(2)}, u32[]{:S(2)}) collective-permute-start(f32[1,8,32]{1,2,0:T(8,128)S(1)} %get-tuple-element.239), channel_id=1, source_target_pairs={{0,4},{4,8},{8,12},{12,16},{16,20},{20,24},{24,28},{28,0},{1,5},{5... | collective-permute-start | bytes 3080 | tf_op jit(solution)/shard_map/ppermute | solution.py:20
  145.9 6.5 %collective-permute-start.38 = (f32[1,8,32]{1,2,0:T(8,128)S(1)}, f32[1,8,32]{1,2,0:T(8,128)S(1)}, u32[]{:S(2)}, u32[]{:S(2)}) collective-permute-start(f32[1,8,32]{1,2,0:T(8,128)S(1)} %get-tuple-element.233), channel_id=1, source_target_pairs={{0,4},{4,8},{8,12},{12,16},{16,20},{20,24},{24,28},{28,0},{1,5},{5... | collective-permute-start | bytes 3080 | tf_op jit(solution)/shard_map/ppermute | solution.py:20
  218.1 6.5 %collective-permute-start.66 = (f32[1,8,32]{1,2,0:T(8,128)S(1)}, f32[1,8,32]{1,2,0:T(8,128)S(1)}, u32[]{:S(2)}, u32[]{:S(2)}) collective-permute-start(f32[1,8,32]{1,2,0:T(8,128)S(1)} %get-tuple-element.227), channel_id=1, source_target_pairs={{0,4},{4,8},{8,12},{12,16},{16,20},{20,24},{24,28},{28,0},{1,5},{5... | collective-permute-start | bytes 3080 | tf_op jit(solution)/shard_map/ppermute | solution.py:20
  224.9 6.5 %collective-permute-start.68 = (f32[1,8,32]{1,2,0:T(8,128)S(1)}, f32[1,8,32]{1,2,0:T(8,128)S(1)}, u32[]{:S(2)}, u32[]{:S(2)}) collective-permute-start(f32[1,8,32]{1,2,0:T(8,128)S(1)} %get-tuple-element.221), channel_id=1, source_target_pairs={{0,4},{4,8},{8,12},{12,16},{16,20},{20,24},{24,28},{28,0},{1,5},{5... | collective-permute-start | bytes 3080 | tf_op jit(solution)/shard_map/ppermute | solution.py:20
  334.9 6.5 %collective-permute-start.106 = (f32[1,8,32]{1,2,0:T(8,128)S(1)}, f32[1,8,32]{1,2,0:T(8,128)S(1)}, u32[]{:S(2)}, u32[]{:S(2)}) collective-permute-start(f32[1,8,32]{1,2,0:T(8,128)S(1)} %get-tuple-element.185), channel_id=1, source_target_pairs={{0,4},{4,8},{8,12},{12,16},{16,20},{20,24},{24,28},{28,0},{1,5},{5... | collective-permute-start | bytes 3080 | tf_op jit(solution)/shard_map/ppermute | solution.py:20
  341.7 6.5 %collective-permute-start.108 = (f32[1,8,32]{1,2,0:T(8,128)S(1)}, f32[1,8,32]{1,2,0:T(8,128)S(1)}, u32[]{:S(2)}, u32[]{:S(2)}) collective-permute-start(f32[1,8,32]{1,2,0:T(8,128)S(1)} %get-tuple-element.179), channel_id=1, source_target_pairs={{0,4},{4,8},{8,12},{12,16},{16,20},{20,24},{24,28},{28,0},{1,5},{5... | collective-permute-start | bytes 3080 | tf_op jit(solution)/shard_map/ppermute | solution.py:20
  408.2 6.5 %collective-permute-start.128 = (f32[1,8,32]{1,2,0:T(8,128)S(1)}, f32[1,8,32]{1,2,0:T(8,128)S(1)}, u32[]{:S(2)}, u32[]{:S(2)}) collective-permute-start(f32[1,8,32]{1,2,0:T(8,128)S(1)} %get-tuple-element.173), channel_id=1, source_target_pairs={{0,4},{4,8},{8,12},{12,16},{16,20},{20,24},{24,28},{28,0},{1,5},{5... | collective-permute-start | bytes 3080 | tf_op jit(solution)/shard_map/ppermute | solution.py:20
  415.0 6.5 %collective-permute-start.130 = (f32[1,8,32]{1,2,0:T(8,128)S(1)}, f32[1,8,32]{1,2,0:T(8,128)S(1)}, u32[]{:S(2)}, u32[]{:S(2)}) collective-permute-start(f32[1,8,32]{1,2,0:T(8,128)S(1)} %get-tuple-element.167), channel_id=1, source_target_pairs={{0,4},{4,8},{8,12},{12,16},{16,20},{20,24},{24,28},{28,0},{1,5},{5... | collective-permute-start | bytes 3080 | tf_op jit(solution)/shard_map/ppermute | solution.py:20
  (126 other events, 573.2 us)
where the time goes:
time: 463 us; the launch traced here: 462 us
  waiting for transfers between devices  240 us (52%)
  starting transfers between devices  148 us (32%)
  local copies, waits for them, and re-layouts  29.1 us (6%)
  other arithmetic  16.9 us (4%)
  blocking collectives  15.7 us (3%)
  matrix products  11 us (2%)
    ppermute x74, waiting for transfers between devices, with_halo(): before = lax.ppermute(last, axis, up)  157 us
    ppermute x74, starting transfers between devices, with_halo(): before = lax.ppermute(last, axis, up)  95 us
    ppermute x74, waiting for transfers between devices, with_halo(): after = lax.ppermute(initial, axis, down)  83.5 us
    ppermute x74, starting transfers between devices, with_halo(): after = lax.ppermute(initial, axis, down)  52.5 us
    reshape x8, local copies, waits for them, and re-layouts, restrict(): values.reshape(extent[0] // 2, 2, extent[1] // 2, 2, extent[2] // 2, 2)  18.4 us
    all_gather x2, blocking collectives, descend(): coarse_source = lax.all_gather(coarse_source, 'gy', axis=1, tiled=True)  10.6 us
    dot_general x16, matrix products, one_plane(): return jnp.dot(one_hot, entries, precision=lax.Precision.HIGHEST)  10.2 us
  transfers between devices with their start and end apart: 148, of which 130 were waited for; matrix products, arithmetic and copies ran while one was open for 8% of the time, Pallas kernels for 0%

commit v1 on v0

v1 whole, which is shorter than its diff:
```python
import functools

import jax
import jax.numpy as jnp
from jax import lax
from jax.experimental import pallas as pl
from jax.experimental.pallas import tpu as pltpu
from jax.sharding import PartitionSpec as P

CYCLES = 2
COARSE = 6
RELAX_WEIGHT = 0.8
KEEP = 1.0 - RELAX_WEIGHT
BLOCK = 4
SIDE = 3
MESH = pl.DeviceIdType.MESH

XL, XH, YL, YH, ZL, ZH, KI, W0, WM, WL = range(10)


def roll(values, shift, axis):
    return pltpu.roll(values, shift % values.shape[axis], axis)


def harmonic(near_k, far_k):
    return 2.0 * near_k * far_k / (near_k + far_k)


def pair_sum(values, stride, axis):
    index = lax.broadcasted_iota(jnp.int32, values.shape, axis)
    odd = (index & stride) != 0
    other = jnp.where(odd, roll(values, stride, axis), roll(values, -stride, axis))
    return values + other


def block_sum(values, sy, sx):
    rows = values.shape[0]
    halved = jnp.concatenate(
        [values[j : j + 1] + values[j + 1 : j + 2] for j in range(0, rows, 2)], axis=0
    )
    return pair_sum(pair_sum(halved, sy, 1), sx, 2)


def doubled(values):
    rows = values.shape[0]
    return jnp.concatenate([values[j // 2 : j // 2 + 1] for j in range(2 * rows)], axis=0)


class Level:
    def __init__(self, faces, kappa, scale, blocks, rpb, u, sy, sx, periodic):
        self.faces, self.kappa, self.scale = faces, kappa, scale
        self.blocks, self.rpb, self.u = blocks, rpb, u
        self.sy, self.sx, self.periodic = sy, sx, periodic

    def loop(self, body, low=0, high=None):
        high = self.blocks if high is None else high

        def step(i, carry):
            body(i * self.u)
            return carry

        lax.fori_loop(low // self.u, high // self.u, step, 0)

    def ghosts(self, ref):
        if self.periodic:
            rows = self.blocks * self.rpb
            ref[0:1] = ref[rows : rows + 1]
            ref[rows + 1 : rows + 2] = ref[1:2]

    def build(self):
        faces, rpb, u = self.faces, self.rpb, self.u

        def body(b):
            k = self.kappa[pl.ds(b + 1, u)] * self.scale
            below = self.kappa[pl.ds(b, u)] * self.scale
            above = self.kappa[pl.ds(b + 2, u)] * self.scale
            row = lax.broadcasted_iota(jnp.int32, k.shape, 1)
            col = lax.broadcasted_iota(jnp.int32, k.shape, 2)
            y_size, x_size = k.shape[1], k.shape[2]
            sy, sx = self.sy, self.sx
            xl = jnp.where(col < sx, 0.0, harmonic(k, roll(k, sx, 2)))
            xh = jnp.where(col >= x_size - sx, 0.0, harmonic(k, roll(k, -sx, 2)))
            yl = jnp.where(row < sy, 0.0, harmonic(k, roll(k, sy, 1)))
            yh = jnp.where(row >= y_size - sy, 0.0, harmonic(k, roll(k, -sy, 1)))
            zl = harmonic(k, below)
            zh = harmonic(k, above)
            base = 1.0 + xl + xh + yl + yh
            at = pl.ds(b, u)
            for name, value in ((XL, xl), (XH, xh), (YL, yl), (YH, yh), (ZL, zl), (ZH, zh), (KI, k)):
                faces[name, at] = value
            if rpb == 1:
                faces[W0, at] = RELAX_WEIGHT / (base + zl + zh)
            else:
                faces[W0, at] = RELAX_WEIGHT / (base + zl + k)
                faces[WL, at] = RELAX_WEIGHT / (base + zh + k)
                if rpb > 2:
                    faces[WM, at] = RELAX_WEIGHT / (base + k + k)

        self.loop(body)

    def weight(self, b):
        at = pl.ds(b, self.u)
        if self.rpb == 1:
            return self.faces[W0, at]
        middle = [self.faces[WM, at]] * (self.rpb - 2) if self.rpb > 2 else []
        return jnp.concatenate([self.faces[W0, at], *middle, self.faces[WL, at]], axis=0)

    def z_faces(self, b):
        at = pl.ds(b, self.u)
        low, high = self.faces[ZL, at], self.faces[ZH, at]
        if self.rpb == 1:
            return low, high
        inner = [self.faces[KI, at]] * (self.rpb - 1)
        return jnp.concatenate([low, *inner], axis=0), jnp.concatenate([*inner, high], axis=0)

    def terms(self, src, b):
        n = self.u * self.rpb
        ext = src[pl.ds(b * self.rpb, n + 2)]
        centre = ext[1 : n + 1]
        at = pl.ds(b, self.u)
        low, high = self.z_faces(b)
        pairs = [
            (low, ext[:n]),
            (high, ext[2:]),
            (self.faces[YL, at], roll(centre, self.sy, 1)),
            (self.faces[YH, at], roll(centre, -self.sy, 1)),
            (self.faces[XL, at], roll(centre, self.sx, 2)),
            (self.faces[XH, at], roll(centre, -self.sx, 2)),
        ]
        return centre, pairs

    def rows(self, b, shift=0):
        return pl.ds(b * self.rpb + shift, self.u * self.rpb)

    def first(self, dst, source):
        def body(b):
            dst[self.rows(b, 1)] = self.weight(b) * source[self.rows(b)]

        self.loop(body)
        self.ghosts(dst)

    def relax(self, dst, src, source, low=0, high=None):
        def body(b):
            centre, pairs = self.terms(src, b)
            total = source[self.rows(b)]
            for face, value in pairs:
                total = total + face * value
            dst[self.rows(b, 1)] = KEEP * centre + self.weight(b) * total

        self.loop(body, low, high)
        self.ghosts(dst)

    def restricted(self, src, source, b):
        centre, pairs = self.terms(src, b)
        rest = source[self.rows(b)] - centre
        for face, value in pairs:
            rest = rest - face * (centre - value)
        return block_sum(rest, self.sy, self.sx) * 0.125

    def restrict(self, dst, src, source, low=0, high=None):
        half = self.u * self.rpb // 2

        def body(b):
            dst[pl.ds(b * self.rpb // 2, half)] = self.restricted(src, source, b)

        self.loop(body, low, high)

    def correct(self, dst, coarse, low=0, high=None):
        half = self.u * self.rpb // 2

        def body(b):
            fine = self.rows(b, 1)
            dst[fine] = dst[fine] + doubled(coarse[pl.ds(b * self.rpb // 2 + 1, half)])

        self.loop(body, low, high)
        self.ghosts(dst)


def kernel(
    gz, gy, conc, phases, grains, grain_class, diffusivity, out,
    c_all, k_all, va, vb, vn, g1, v1a, v1b, rest, spread,
    k2, g2, v2a, v2b, k3, g3, v3a, v3b, k4, g4, v4a, v4b, f0, f1, f2, f3, f4,
    c_send, c_recv, k_send, k_recv, k2_send, k2_recv, g2_send, g2_recv, v_send, v_recv,
):
    my_z, my_y = lax.axis_index("gz"), lax.axis_index("gy")
    z_len, y_len = conc.shape[0], conc.shape[1]
    own = z_len // BLOCK
    blocks = own + 2 * SIDE
    halo = SIDE * BLOCK
    nz2 = k2.shape[0] - 2
    y2 = k2.shape[1]
    zs = [lax.rem(my_z + o, gz) for o in range(gz)]
    ys = [lax.rem(my_y + o, gy) for o in range(gy)]

    barrier = pltpu.get_barrier_semaphore()
    greeted = [(zs[0], ys[o]) for o in range(1, gy)]
    greeted += [(zs[o], ys[j]) for o in (1, gz - 1) for j in range(gy)]
    greeted += [(zs[o], ys[0]) for o in range(2, gz - 1)]
    for device in greeted:
        pl.semaphore_signal(barrier, inc=1, device_id=device, device_id_type=MESH)

    y_rows = pl.ds(pl.multiple_of(my_y * y_len, y_len), y_len)
    for b in range(own):
        grain, phase = grains[b * BLOCK], phases[b * BLOCK]

        def pick_class(i, cls):
            return jnp.where(grain == i, grain_class[i], cls)

        cls = lax.fori_loop(0, grain_class.shape[0], pick_class, jnp.zeros_like(grain))
        kappa = jnp.zeros(grain.shape, jnp.float32)
        for p in range(diffusivity.shape[0]):
            for c in range(diffusivity.shape[1]):
                kappa = jnp.where((phase == p) & (cls == c), diffusivity[p, c], kappa)
        k_all[1 + SIDE + b, y_rows] = kappa
    c_all[pl.ds(halo, z_len), y_rows] = conc[...]

    pl.semaphore_wait(barrier, len(greeted))

    sends = []

    def send(src, dst, send_sem, recv_sem, device):
        copy = pltpu.make_async_remote_copy(
            src_ref=src, dst_ref=dst, send_sem=send_sem, recv_sem=recv_sem,
            device_id=device, device_id_type=MESH,
        )
        copy.start()
        sends.append(copy)
        return copy

    first_round = []
    plans = [(zs[0], o, 0, z_len, halo) for o in range(1, gy)]
    plans += [(zs[1], o, z_len - halo, halo, 0) for o in range(gy)]
    plans += [(zs[gz - 1], o, 0, halo, halo + z_len) for o in range(gy)]
    for n, (z, o, start, length, to) in enumerate(plans):
        first_round.append(send(
            k_all.at[pl.ds(1 + SIDE + start // BLOCK, length // BLOCK), y_rows],
            k_all.at[pl.ds(1 + to // BLOCK, length // BLOCK), y_rows],
            k_send.at[n], k_recv.at[n], (z, ys[o]),
        ))
    fields = []
    for n, (z, o, start, length, to) in enumerate(plans):
        fields.append(send(
            conc.at[pl.ds(start, length)],
            c_all.at[pl.ds(to, length), y_rows],
            c_send.at[n], c_recv.at[n], (z, ys[o]),
        ))

    for copy in first_round:
        copy.wait_recv()
    k_all[0:1] = k_all[1:2]
    k_all[blocks + 1 : blocks + 2] = k_all[blocks : blocks + 1]

    z2_rows = pl.ds(own * my_z, own)
    z2_rows_padded = pl.ds(1 + own * my_z, own)
    for b in range(own):
        k2[1 + own * my_z + b] = (
            k_all.at[1 + SIDE + b][pl.ds(0, y2, stride=BLOCK), :] * 0.25
        )
    second_round = [
        send(
            k2.at[z2_rows_padded], k2.at[z2_rows_padded],
            k2_send.at[o - 1], k2_recv.at[o - 1], (zs[o], ys[0]),
        )
        for o in range(1, gz)
    ]

    u2 = 8
    l0 = Level(f0, k_all, 1.0, blocks, 4, 1, 1, 1, False)
    l1 = Level(f1, k_all, 0.5, blocks, 2, 1, 2, 2, False)
    l2 = Level(f2, k2, 1.0, nz2, 1, u2, 1, 4, True)
    l3 = Level(f3, k3, 1.0, nz2 // 2, 1, u2, 2, 8, True)
    l4 = Level(f4, k4, 1.0, nz2 // 4, 1, u2, 4, 16, True)
    l0.build()
    l1.build()
    for copy in fields:
        copy.wait_recv()

    for cycle in range(CYCLES):
        if cycle == 0:
            l0.first(va, c_all)
        else:
            l0.relax(va, vn, c_all)
        l0.relax(vb, va, c_all)
        l0.restrict(g1, vb, c_all)
        l1.first(v1a, g1)
        l1.relax(v1b, v1a, g1)

        def own_rest(b):
            rest[pl.ds(b - SIDE, 1)] = l1.restricted(v1b, g1, b)

        l1.loop(own_rest, SIDE, SIDE + own)
        source2 = g2.at[cycle]
        for b in range(own):
            source2[own * my_z + b] = rest.at[b][pl.ds(0, y2, stride=BLOCK), :]
        gathered = [
            send(
                source2.at[z2_rows], source2.at[z2_rows],
                g2_send.at[cycle, o - 1], g2_recv.at[cycle, o - 1], (zs[o], ys[0]),
            )
            for o in range(1, gz)
        ]
        if cycle == 0:
            for copy in second_round:
                copy.wait_recv()
            l2.ghosts(k2)
            l2.build()
            for fine, coarse, level in ((k2, k3, l2), (k3, k4, l3)):

                def coarser(b):
                    coarse[pl.ds(b // 2 + 1, u2 // 2)] = (
                        block_sum(fine[pl.ds(b + 1, u2)], level.sy, level.sx) * 0.0625
                    )

                level.loop(coarser)
                above = l3 if level is l2 else l4
                above.ghosts(coarse)
                above.build()
        for copy in gathered:
            copy.wait_recv()

        l2.first(v2a, source2)
        l2.relax(v2b, v2a, source2)
        l2.restrict(g3, v2b, source2)
        l3.first(v3a, g3)
        l3.relax(v3b, v3a, g3)
        l3.restrict(g4, v3b, g3)
        l4.first(v4a, g4)
        here, there = v4a, v4b
        for _ in range(COARSE - 1):
            l4.relax(there, here, g4)
            here, there = there, here
        l3.correct(v3b, here)
        l3.relax(v3a, v3b, g3)
        l3.relax(v3b, v3a, g3)
        l2.correct(v2b, v3b)
        l2.relax(v2a, v2b, source2)
        l2.relax(v2b, v2a, source2)

        def widen(b):
            z = lax.rem(own * my_z + b - SIDE + nz2, nz2)
            value = v2b[z + 1]
            target = spread.at[b + 1]
            for k in range(BLOCK):
                target[pl.ds(k, y2, stride=BLOCK), :] = value

        l1.loop(widen, 1, blocks - 1)
        l1.correct(v1b, spread, 1, blocks - 1)
        l1.relax(v1a, v1b, g1, 1, blocks - 1)
        l1.relax(v1b, v1a, g1, 1, blocks - 1)
        l0.correct(vb, v1b, 2, blocks - 2)
        l0.relax(va, vb, c_all, 2, blocks - 2)
        if cycle < CYCLES - 1:
            l0.relax(vn, va, c_all, SIDE, SIDE + own)
            halves = [
                send(
                    vn.at[pl.ds(1 + z_len, halo)], vn.at[pl.ds(1, halo)],
                    v_send.at[0], v_recv.at[0], (zs[1], ys[0]),
                ),
                send(
                    vn.at[pl.ds(1 + halo, halo)], vn.at[pl.ds(1 + halo + z_len, halo)],
                    v_send.at[1], v_recv.at[1], (zs[gz - 1], ys[0]),
                ),
            ]
            for copy in halves:
                copy.wait_recv()
        else:
            l0.relax(vb, va, c_all, SIDE, SIDE + own)
    out[...] = vb[pl.ds(1 + halo, z_len), y_rows]

    for copy in sends:
        copy.wait_send()


def per_device(gz, gy, concentration, phases, grains, grain_class, diffusivity):
    z_len, y_len, x_len = concentration.shape
    blocks = z_len // BLOCK + 2 * SIDE
    y_all = y_len * gy
    y2 = y_all // BLOCK
    nz2 = z_len // BLOCK * gz
    z_all = blocks * BLOCK
    near = 3 * gy - 1

    def vmem(*shape):
        return pltpu.VMEM(shape + (x_len,), jnp.float32)

    def sems(*shape):
        return pltpu.SemaphoreType.DMA(shape)

    scratch = [
        vmem(z_all, y_all), vmem(blocks + 2, y_all),
        vmem(z_all + 2, y_all), vmem(z_all + 2, y_all), vmem(z_all + 2, y_all),
        vmem(z_all // 2, y_all), vmem(z_all // 2 + 2, y_all), vmem(z_all // 2 + 2, y_all),
        vmem(z_len // BLOCK, y_all), vmem(blocks + 2, y_all),
        vmem(nz2 + 2, y2), vmem(CYCLES, nz2, y2), vmem(nz2 + 2, y2), vmem(nz2 + 2, y2),
    ]
    for rows in (nz2 // 2, nz2 // 4):
        scratch += [vmem(rows + 2, y2), vmem(rows, y2), vmem(rows + 2, y2), vmem(rows + 2, y2)]
    scratch += [vmem(10, blocks, y_all), vmem(10, blocks, y_all)]
    scratch += [vmem(8, rows, y2) for rows in (nz2, nz2 // 2, nz2 // 4)]
    scratch += [sems(near)] * 4 + [sems(gz - 1)] * 2 + [sems(CYCLES, gz - 1)] * 2 + [sems(2)] * 2
    in_vmem = pl.BlockSpec(memory_space=pltpu.VMEM)
    in_smem = pl.BlockSpec(memory_space=pltpu.SMEM)
    return pl.pallas_call(
        functools.partial(kernel, gz, gy),
        out_shape=jax.ShapeDtypeStruct(concentration.shape, jnp.float32),
        in_specs=[in_vmem, in_vmem, in_vmem, in_smem, in_smem],
        out_specs=in_vmem,
        scratch_shapes=scratch,
        compiler_params=pltpu.CompilerParams(
            collective_id=0, has_side_effects=True, vmem_limit_bytes=40 * 1024 * 1024
        ),
    )(concentration, phases, grains, grain_class, diffusivity)


def solution(mesh):
    placed = (P("gz", "gy", None), P("gz", "gy", None), P("gz", "gy", None), P(), P())
    body = functools.partial(per_device, mesh.shape["gz"], mesh.shape["gy"])
    return jax.shard_map(
        body, mesh=mesh, in_specs=placed, out_specs=P("gz", "gy", None), check_vma=False
    )
```

time: 463 us -> 66.3 us (0.14)
  waiting for transfers between devices: 240 us -> 0 us
  starting transfers between devices: 148 us -> 0 us
  Pallas kernels: 0 us -> 61.5 us
  local copies, waits for them, and re-layouts: 29.1 us -> 4.48 us
  other arithmetic: 16.9 us -> 0 us
  blocking collectives: 15.7 us -> 0 us
  matrix products: 11 us -> 0 us
    ppermute x148 -> x0, waiting for transfers between devices: 240 us -> none  [the longest x74 157 us: with_halo(): before = lax.ppermute(last, axis, up)]
    ppermute x148 -> x0, starting transfers between devices: 148 us -> none  [the longest x74 95 us: with_halo(): before = lax.ppermute(last, axis, up)]
    pallas_call x0 -> x1, Pallas kernels: none -> 61.5 us  [per_device(): pl.pallas_call(functools.partial(kernel, gz, gy), out_shape=jax.ShapeDtyp...]
    reshape x19 -> x0, local copies, waits for them, and re-layouts: 19.6 us -> none  [the longest x8 18.4 us: restrict(): values.reshape(extent[0] // 2, 2, extent[1] // 2, 2, extent[2] // 2, 2)]
    all_gather x3 -> x0, blocking collectives: 15.7 us -> none  [the longest x2 10.6 us: descend(): coarse_source = lax.all_gather(coarse_source, 'gy', axis=1, tiled=True)]
    dot_general x17 -> x0, matrix products: 11 us -> none  [the longest x16 10.2 us: one_plane(): return jnp.dot(one_hot, entries, precision=lax.Precision.HIGHEST)]
    reduce_sum x15 -> x0, other arithmetic: 8.81 us -> none  [restrict(): values.reshape(extent[0] // 2, 2, extent[1] // 2, 2, extent[2] // 2, 2)]
    slice x165 -> x0, local copies, waits for them, and re-layouts: 7.13 us -> none  [the longest x51 2.71 us: apply_operator(): jnp.roll(centre, -1, 2)]
  transfers between devices with their start and end apart: 148 -> 0, of which waited for: 130 -> 0; matrix products, arithmetic and copies ran while one was open for 8% -> 0% of each run, Pallas kernels for 0% -> 0%
where the time goes in v1:
time: 66.3 us; the launch traced here: 66 us
  Pallas kernels  61.5 us (93%)
  local copies, waits for them, and re-layouts  4.48 us (7%)
    pallas_call x1, Pallas kernels, per_device(): pl.pallas_call(functools.partial(kernel, gz, gy), out_shape=jax.ShapeDtyp...  61.5 us
    unnamed x11, local copies, waits for them, and re-layouts  4.48 us

profile of v1, /device:TPU:0, one launch (start us, length us, event | category | flops | bytes accessed | tf_op | source)
XLA Modules:
  0.0 66.0 jit_solution(4199021125406885961)
XLA Ops:
  0.0 0.0 copy-start
  0.0 0.8 %copy-done = f32[16,8,128]{2,1,0:T(8,128)S(1)} copy-done((f32[16,8,128]{2,1,0:T(8,128)S(1)}, f32[16,8,128]{2,1,0:T(8,128)}, u32[]{:S(2)}) %copy-start) | copy-done | bytes 65560
  0.8 0.0 copy-start.1
  0.8 0.8 %copy-done.1 = s32[16,8,128]{2,1,0:T(8,128)S(1)} copy-done((s32[16,8,128]{2,1,0:T(8,128)S(1)}, s32[16,8,128]{2,1,0:T(8,128)}, u32[]{:S(2)}) %copy-start.1) | copy-done | bytes 65560
  1.7 0.0 copy-start.2
  1.7 0.8 %copy-done.2 = s32[16,8,128]{2,1,0:T(8,128)S(1)} copy-done((s32[16,8,128]{2,1,0:T(8,128)S(1)}, s32[16,8,128]{2,1,0:T(8,128)}, u32[]{:S(2)}) %copy-start.2) | copy-done | bytes 65560
  2.5 0.0 copy-start.3
  2.5 0.7 %copy-done.3 = f32[3,4]{1,0:T(4,128)S(1)} copy-done((f32[3,4]{1,0:T(4,128)S(1)}, f32[3,4]{1,0:T(4,128)}, u32[]{:S(2)}) %copy-start.3) | copy-done | bytes 72
  3.2 0.0 copy-start.4
  3.2 0.7 copy-done.4
  3.9 61.5 %shard_map.55 = f32[16,8,128]{2,1,0:T(8,128)S(1)} custom-call(f32[16,8,128]{2,1,0:T(8,128)S(1)} %copy-done, s32[16,8,128]{2,1,0:T(8,128)S(1)} %copy-done.1, s32[16,8,128]{2,1,0:T(8,128)S(1)} %copy-done.2, s32[64]{0:T(128)S(1)} %copy-done.4, f32[3,4]{1,0:T(4,128)S(1)} %copy-done.3), custom_call_target="tpu_custom_call" | custom-call | tf_op jit(solution)/shard_map/pallas_call | solution.py:403
  65.3 0.6 copy.7
Async XLA Ops:
  0.0 0.8 %copy-start = (f32[16,8,128]{2,1,0:T(8,128)S(1)}, f32[16,8,128]{2,1,0:T(8,128)}, u32[]{:S(2)}) copy-start(f32[16,8,128]{2,1,0:T(8,128)} %conc.1) | copy-start | bytes 196612
  0.8 0.8 %copy-start.1 = (s32[16,8,128]{2,1,0:T(8,128)S(1)}, s32[16,8,128]{2,1,0:T(8,128)}, u32[]{:S(2)}) copy-start(s32[16,8,128]{2,1,0:T(8,128)} %phases.1) | copy-start | bytes 196612
  1.7 0.8 %copy-start.2 = (s32[16,8,128]{2,1,0:T(8,128)S(1)}, s32[16,8,128]{2,1,0:T(8,128)}, u32[]{:S(2)}) copy-start(s32[16,8,128]{2,1,0:T(8,128)} %grains.1) | copy-start | bytes 196612
  2.5 0.7 %copy-start.3 = (f32[3,4]{1,0:T(4,128)S(1)}, f32[3,4]{1,0:T(4,128)}, u32[]{:S(2)}) copy-start(f32[3,4]{1,0:T(4,128)} %diffusivity.1) | copy-start | bytes 148
  3.2 0.7 copy-start.4

commit v2 on v1

--- a/solution.py
+++ b/solution.py
@@ -56,10 +56,10 @@
         high = self.blocks if high is None else high
 
         def step(i, carry):
-            body(i * self.u)
+            body(low + i * self.u)
             return carry
 
-        lax.fori_loop(low // self.u, high // self.u, step, 0)
+        lax.fori_loop(0, (high - low) // self.u, step, 0)
 
     def ghosts(self, ref):
         if self.periodic:
@@ -99,33 +99,47 @@
         self.loop(body)
 
     def weight(self, b):
+        if self.rpb == 1:
+            return self.faces[W0, pl.ds(b, self.u)]
+        parts = []
+        for j in range(self.u):
+            at = pl.ds(b + j, 1)
+            middle = [self.faces[WM, at]] * (self.rpb - 2) if self.rpb > 2 else []
+            parts += [self.faces[W0, at], *middle, self.faces[WL, at]]
+        return jnp.concatenate(parts, axis=0)
+
+    def face(self, name, b):
+        if self.rpb == 1 or self.u == 1:
+            return self.faces[name, pl.ds(b, self.u)]
+        parts = []
+        for j in range(self.u):
+            parts += [self.faces[name, pl.ds(b + j, 1)]] * self.rpb
+        return jnp.concatenate(parts, axis=0)
+
+    def z_faces(self, b):
         at = pl.ds(b, self.u)
         if self.rpb == 1:
-            return self.faces[W0, at]
-        middle = [self.faces[WM, at]] * (self.rpb - 2) if self.rpb > 2 else []
-        return jnp.concatenate([self.faces[W0, at], *middle, self.faces[WL, at]], axis=0)
-
-    def z_faces(self, b):
-        at = pl.ds(b, self.u)
-        low, high = self.faces[ZL, at], self.faces[ZH, at]
-        if self.rpb == 1:
-            return low, high
-        inner = [self.faces[KI, at]] * (self.rpb - 1)
-        return jnp.concatenate([low, *inner], axis=0), jnp.concatenate([*inner, high], axis=0)
+            return self.faces[ZL, at], self.faces[ZH, at]
+        low, high = [], []
+        for j in range(self.u):
+            at = pl.ds(b + j, 1)
+            inner = [self.faces[KI, at]] * (self.rpb - 1)
+            low += [self.faces[ZL, at], *inner]
+            high += [*inner, self.faces[ZH, at]]
+        return jnp.concatenate(low, axis=0), jnp.concatenate(high, axis=0)
 
     def terms(self, src, b):
         n = self.u * self.rpb
         ext = src[pl.ds(b * self.rpb, n + 2)]
         centre = ext[1 : n + 1]
-        at = pl.ds(b, self.u)
         low, high = self.z_faces(b)
         pairs = [
             (low, ext[:n]),
             (high, ext[2:]),
-            (self.faces[YL, at], roll(centre, self.sy, 1)),
-            (self.faces[YH, at], roll(centre, -self.sy, 1)),
-            (self.faces[XL, at], roll(centre, self.sx, 2)),
-            (self.faces[XH, at], roll(centre, -self.sx, 2)),
+            (self.face(YL, b), roll(centre, self.sy, 1)),
+            (self.face(YH, b), roll(centre, -self.sy, 1)),
+            (self.face(XL, b), roll(centre, self.sx, 2)),
+            (self.face(XH, b), roll(centre, -self.sx, 2)),
         ]
         return centre, pairs
 
@@ -181,6 +195,7 @@
     c_all, k_all, va, vb, vn, g1, v1a, v1b, rest, spread,
     k2, g2, v2a, v2b, k3, g3, v3a, v3b, k4, g4, v4a, v4b, f0, f1, f2, f3, f4,
     c_send, c_recv, k_send, k_recv, k2_send, k2_recv, g2_send, g2_recv, v_send, v_recv,
+    in_sem, grain_in, phase_in,
 ):
     my_z, my_y = lax.axis_index("gz"), lax.axis_index("gy")
     z_len, y_len = conc.shape[0], conc.shape[1]
@@ -200,19 +215,29 @@
         pl.semaphore_signal(barrier, inc=1, device_id=device, device_id_type=MESH)
 
     y_rows = pl.ds(pl.multiple_of(my_y * y_len, y_len), y_len)
+    loads = [
+        pltpu.make_async_copy(conc, c_all.at[pl.ds(halo, z_len), y_rows], in_sem.at[0]),
+    ]
     for b in range(own):
-        grain, phase = grains[b * BLOCK], phases[b * BLOCK]
-
-        def pick_class(i, cls):
-            return jnp.where(grain == i, grain_class[i], cls)
-
-        cls = lax.fori_loop(0, grain_class.shape[0], pick_class, jnp.zeros_like(grain))
-        kappa = jnp.zeros(grain.shape, jnp.float32)
-        for p in range(diffusivity.shape[0]):
-            for c in range(diffusivity.shape[1]):
-                kappa = jnp.where((phase == p) & (cls == c), diffusivity[p, c], kappa)
-        k_all[1 + SIDE + b, y_rows] = kappa
-    c_all[pl.ds(halo, z_len), y_rows] = conc[...]
+        loads += [
+            pltpu.make_async_copy(grains.at[b * BLOCK], grain_in.at[b], in_sem.at[1 + 2 * b]),
+            pltpu.make_async_copy(phases.at[b * BLOCK], phase_in.at[b], in_sem.at[2 + 2 * b]),
+        ]
+    for copy in loads:
+        copy.start()
+    for copy in loads:
+        copy.wait()
+    grain, phase = grain_in[...], phase_in[...]
+    cls = jnp.zeros_like(grain)
+    for i in range(grain_class.shape[0]):
+        cls = jnp.where(grain == i, grain_class[i], cls)
+    classes = diffusivity.shape[1]
+    label = phase * classes + cls
+    kappa = jnp.zeros(grain.shape, jnp.float32)
+    for p in range(diffusivity.shape[0]):
+        for c in range(classes):
+            kappa = jnp.where(label == p * classes + c, diffusivity[p, c], kappa)
+    k_all[pl.ds(1 + SIDE, own), y_rows] = kappa
 
     pl.semaphore_wait(barrier, len(greeted))
 
@@ -238,9 +263,13 @@
             k_send.at[n], k_recv.at[n], (z, ys[o]),
         ))
     fields = []
+    near = halo - 2
+    plans = [(zs[0], o, 0, z_len, halo) for o in range(1, gy)]
+    plans += [(zs[1], o, z_len - near, near, halo - near) for o in range(gy)]
+    plans += [(zs[gz - 1], o, 0, near, halo + z_len) for o in range(gy)]
     for n, (z, o, start, length, to) in enumerate(plans):
         fields.append(send(
-            conc.at[pl.ds(start, length)],
+            c_all.at[pl.ds(halo + start, length), y_rows],
             c_all.at[pl.ds(to, length), y_rows],
             c_send.at[n], c_recv.at[n], (z, ys[o]),
         ))
@@ -264,12 +293,12 @@
         for o in range(1, gz)
     ]
 
-    u2 = 8
+    u2, u3, u4 = [min(16, nz2 // m) for m in (1, 2, 4)]
     l0 = Level(f0, k_all, 1.0, blocks, 4, 1, 1, 1, False)
-    l1 = Level(f1, k_all, 0.5, blocks, 2, 1, 2, 2, False)
+    l1 = Level(f1, k_all, 0.5, blocks, 2, 2, 2, 2, False)
     l2 = Level(f2, k2, 1.0, nz2, 1, u2, 1, 4, True)
-    l3 = Level(f3, k3, 1.0, nz2 // 2, 1, u2, 2, 8, True)
-    l4 = Level(f4, k4, 1.0, nz2 // 4, 1, u2, 4, 16, True)
+    l3 = Level(f3, k3, 1.0, nz2 // 2, 1, u3, 2, 8, True)
+    l4 = Level(f4, k4, 1.0, nz2 // 4, 1, u4, 4, 16, True)
     l0.build()
     l1.build()
     for copy in fields:
@@ -286,7 +315,7 @@
         l1.relax(v1b, v1a, g1)
 
         def own_rest(b):
-            rest[pl.ds(b - SIDE, 1)] = l1.restricted(v1b, g1, b)
+            rest[pl.ds(b - SIDE, l1.u)] = l1.restricted(v1b, g1, b)
 
         l1.loop(own_rest, SIDE, SIDE + own)
         source2 = g2.at[cycle]
@@ -307,8 +336,8 @@
             for fine, coarse, level in ((k2, k3, l2), (k3, k4, l3)):
 
                 def coarser(b):
-                    coarse[pl.ds(b // 2 + 1, u2 // 2)] = (
-                        block_sum(fine[pl.ds(b + 1, u2)], level.sy, level.sx) * 0.0625
+                    coarse[pl.ds(b // 2 + 1, level.u // 2)] = (
+                        block_sum(fine[pl.ds(b + 1, level.u)], level.sy, level.sx) * 0.0625
                     )
 
                 level.loop(coarser)
@@ -336,14 +365,13 @@
         l2.relax(v2a, v2b, source2)
         l2.relax(v2b, v2a, source2)
 
-        def widen(b):
+        for b in range(1, blocks - 1):
             z = lax.rem(own * my_z + b - SIDE + nz2, nz2)
             value = v2b[z + 1]
             target = spread.at[b + 1]
             for k in range(BLOCK):
                 target[pl.ds(k, y2, stride=BLOCK), :] = value
 
-        l1.loop(widen, 1, blocks - 1)
         l1.correct(v1b, spread, 1, blocks - 1)
         l1.relax(v1a, v1b, g1, 1, blocks - 1)
         l1.relax(v1b, v1a, g1, 1, blocks - 1)
@@ -353,11 +381,12 @@
             l0.relax(vn, va, c_all, SIDE, SIDE + own)
             halves = [
                 send(
-                    vn.at[pl.ds(1 + z_len, halo)], vn.at[pl.ds(1, halo)],
+                    vn.at[pl.ds(2 + z_len, halo - 1)], vn.at[pl.ds(2, halo - 1)],
                     v_send.at[0], v_recv.at[0], (zs[1], ys[0]),
                 ),
                 send(
-                    vn.at[pl.ds(1 + halo, halo)], vn.at[pl.ds(1 + halo + z_len, halo)],
+                    vn.at[pl.ds(1 + halo, halo - 1)],
+                    vn.at[pl.ds(1 + halo + z_len, halo - 1)],
                     v_send.at[1], v_recv.at[1], (zs[gz - 1], ys[0]),
                 ),
             ]
@@ -398,16 +427,19 @@
     scratch += [vmem(10, blocks, y_all), vmem(10, blocks, y_all)]
     scratch += [vmem(8, rows, y2) for rows in (nz2, nz2 // 2, nz2 // 4)]
     scratch += [sems(near)] * 4 + [sems(gz - 1)] * 2 + [sems(CYCLES, gz - 1)] * 2 + [sems(2)] * 2
+    planes = (z_len // BLOCK, y_len, x_len)
+    scratch += [sems(1 + 2 * planes[0])] + [pltpu.VMEM(planes, jnp.int32)] * 2
+    in_hbm = pl.BlockSpec(memory_space=pl.ANY)
     in_vmem = pl.BlockSpec(memory_space=pltpu.VMEM)
     in_smem = pl.BlockSpec(memory_space=pltpu.SMEM)
     return pl.pallas_call(
         functools.partial(kernel, gz, gy),
         out_shape=jax.ShapeDtypeStruct(concentration.shape, jnp.float32),
-        in_specs=[in_vmem, in_vmem, in_vmem, in_smem, in_smem],
+        in_specs=[in_hbm, in_hbm, in_hbm, in_smem, in_smem],
         out_specs=in_vmem,
         scratch_shapes=scratch,
         compiler_params=pltpu.CompilerParams(
-            collective_id=0, has_side_effects=True, vmem_limit_bytes=40 * 1024 * 1024
+            collective_id=0, has_side_effects=True, vmem_limit_bytes=60 * 1024 * 1024
         ),
     )(concentration, phases, grains, grain_class, diffusivity)
 

time: 66.3 us -> 57.7 us (0.87)
  Pallas kernels: 61.5 us -> 56 us
  local copies, waits for them, and re-layouts: 4.48 us -> 1.47 us
    pallas_call x1, Pallas kernels: 61.5 us -> 56 us  [per_device(): pl.pallas_call(functools.partial(kernel, gz, gy), out_shape=jax.ShapeDtyp...]
    unnamed x11 -> x1, local copies, waits for them, and re-layouts: 4.48 us -> 1.47 us
where the time goes in v2:
time: 57.7 us; the launch traced here: 57.5 us
  Pallas kernels  56 us (97%)
  local copies, waits for them, and re-layouts  1.47 us (3%)
    pallas_call x1, Pallas kernels, per_device(): pl.pallas_call(functools.partial(kernel, gz, gy), out_shape=jax.ShapeDtyp...  56 us
    unnamed x1, local copies, waits for them, and re-layouts  1.47 us

profile of v2, /device:TPU:0, one launch (start us, length us, event | category | flops | bytes accessed | tf_op | source)
XLA Modules:
  0.0 57.5 jit_solution(16673338628397905634)
XLA Ops:
  0.0 56.0 %shard_map.55 = f32[16,8,128]{2,1,0:T(8,128)} custom-call(f32[16,8,128]{2,1,0:T(8,128)} %conc.1, s32[16,8,128]{2,1,0:T(8,128)} %phases.1, s32[16,8,128]{2,1,0:T(8,128)} %grains.1, s32[64]{0:T(128)} %grain_class.1, f32[3,4]{1,0:T(4,128)} %diffusivity.1), custom_call_target="tpu_custom_call" | custom-call | tf_op jit(solution)/shard_map/pallas_call | solution.py:435
  56.0 1.5 %copy.7 = f32[16,8,128]{2,1,0:T(8,128)} copy(f32[16,8,128]{2,1,0:T(8,128)} %shard_map.55) | data formatting | bytes 131072

commit v3 on v2

--- a/solution.py
+++ b/solution.py
@@ -44,6 +44,23 @@
 def doubled(values):
     rows = values.shape[0]
     return jnp.concatenate([values[j // 2 : j // 2 + 1] for j in range(2 * rows)], axis=0)
+
+
+def pack(rows):
+    col = lax.broadcasted_iota(jnp.int32, rows[0].shape, 1) & (BLOCK - 1)
+    packed = rows[0]
+    for b in range(1, len(rows)):
+        packed = jnp.where(col == b, rows[b], packed)
+    return packed
+
+
+def unpack(dst, packed, count, shift):
+    col = lax.broadcasted_iota(jnp.int32, packed.shape, 2) & (BLOCK - 1)
+    for b in range(count):
+        lanes = jnp.where(col == b, packed, 0.0)
+        values = pair_sum(pair_sum(lanes, 1, 2), 2, 2)
+        for d in range(packed.shape[0]):
+            dst[d * count + b + shift] = values[d]
 
 
 class Level:
@@ -195,7 +212,7 @@
     c_all, k_all, va, vb, vn, g1, v1a, v1b, rest, spread,
     k2, g2, v2a, v2b, k3, g3, v3a, v3b, k4, g4, v4a, v4b, f0, f1, f2, f3, f4,
     c_send, c_recv, k_send, k_recv, k2_send, k2_recv, g2_send, g2_recv, v_send, v_recv,
-    in_sem, grain_in, phase_in,
+    in_sem, grain_in, phase_in, k2_packed, g2_packed,
 ):
     my_z, my_y = lax.axis_index("gz"), lax.axis_index("gy")
     z_len, y_len = conc.shape[0], conc.shape[1]
@@ -262,32 +279,39 @@
             k_all.at[pl.ds(1 + to // BLOCK, length // BLOCK), y_rows],
             k_send.at[n], k_recv.at[n], (z, ys[o]),
         ))
-    fields = []
+    core = lax.rem(my_y, 2)
+    sibling = my_y + 1 - 2 * core
     near = halo - 2
-    plans = [(zs[0], o, 0, z_len, halo) for o in range(1, gy)]
-    plans += [(zs[1], o, z_len - near, near, halo - near) for o in range(gy)]
-    plans += [(zs[gz - 1], o, 0, near, halo + z_len) for o in range(gy)]
-    for n, (z, o, start, length, to) in enumerate(plans):
-        fields.append(send(
-            c_all.at[pl.ds(halo + start, length), y_rows],
-            c_all.at[pl.ds(to, length), y_rows],
-            c_send.at[n], c_recv.at[n], (z, ys[o]),
-        ))
+    fields = [send(
+        c_all.at[pl.ds(halo, z_len), y_rows], c_all.at[pl.ds(halo, z_len), y_rows],
+        c_send.at[0], c_recv.at[0], (zs[0], sibling),
+    )]
+    direct = []
+    spans = [(0, 0, z_len, halo), (1, z_len - near, near, halo - near), (gz - 1, 0, near, halo + z_len)]
+    for dz, start, length, to in spans:
+        for o in range(0, gy, 2):
+            if dz == 0 and o == 0:
+                continue
+            n = 1 + len(direct)
+            copy = send(
+                c_all.at[pl.ds(halo + start, length), y_rows],
+                c_all.at[pl.ds(to, length), y_rows],
+                c_send.at[n], c_recv.at[n], (zs[dz], ys[o]),
+            )
+            came_y = pl.ds(pl.multiple_of(ys[(gy - o) % gy] * y_len, y_len), y_len)
+            direct.append((copy, c_all.at[pl.ds(to, length), came_y]))
 
     for copy in first_round:
         copy.wait_recv()
     k_all[0:1] = k_all[1:2]
     k_all[blocks + 1 : blocks + 2] = k_all[blocks : blocks + 1]
 
-    z2_rows = pl.ds(own * my_z, own)
-    z2_rows_padded = pl.ds(1 + own * my_z, own)
-    for b in range(own):
-        k2[1 + own * my_z + b] = (
-            k_all.at[1 + SIDE + b][pl.ds(0, y2, stride=BLOCK), :] * 0.25
-        )
+    k2_packed[my_z] = pack(
+        [k_all.at[1 + SIDE + b][pl.ds(0, y2, stride=BLOCK), :] * 0.25 for b in range(own)]
+    )
     second_round = [
         send(
-            k2.at[z2_rows_padded], k2.at[z2_rows_padded],
+            k2_packed.at[my_z], k2_packed.at[my_z],
             k2_send.at[o - 1], k2_recv.at[o - 1], (zs[o], ys[0]),
         )
         for o in range(1, gz)
@@ -300,6 +324,10 @@
     l3 = Level(f3, k3, 1.0, nz2 // 2, 1, u3, 2, 8, True)
     l4 = Level(f4, k4, 1.0, nz2 // 4, 1, u4, 4, 16, True)
     l0.build()
+    for n, (copy, came) in enumerate(direct):
+        copy.wait_recv()
+        m = 1 + len(direct) + n
+        fields.append(send(came, came, c_send.at[m], c_recv.at[m], (zs[0], sibling)))
     l1.build()
     for copy in fields:
         copy.wait_recv()
@@ -318,12 +346,12 @@
             rest[pl.ds(b - SIDE, l1.u)] = l1.restricted(v1b, g1, b)
 
         l1.loop(own_rest, SIDE, SIDE + own)
-        source2 = g2.at[cycle]
-        for b in range(own):
-            source2[own * my_z + b] = rest.at[b][pl.ds(0, y2, stride=BLOCK), :]
+        source2 = g2
+        mine = g2_packed.at[cycle, my_z]
+        mine[...] = pack([rest.at[b][pl.ds(0, y2, stride=BLOCK), :] for b in range(own)])
         gathered = [
             send(
-                source2.at[z2_rows], source2.at[z2_rows],
+                mine, mine,
                 g2_send.at[cycle, o - 1], g2_recv.at[cycle, o - 1], (zs[o], ys[0]),
             )
             for o in range(1, gz)
@@ -331,6 +359,7 @@
         if cycle == 0:
             for copy in second_round:
                 copy.wait_recv()
+            unpack(k2, k2_packed[...], own, 1)
             l2.ghosts(k2)
             l2.build()
             for fine, coarse, level in ((k2, k3, l2), (k3, k4, l3)):
@@ -346,6 +375,7 @@
                 above.build()
         for copy in gathered:
             copy.wait_recv()
+        unpack(g2, g2_packed[cycle], own, 0)
 
         l2.first(v2a, source2)
         l2.relax(v2b, v2a, source2)
@@ -379,18 +409,24 @@
         l0.relax(va, vb, c_all, 2, blocks - 2)
         if cycle < CYCLES - 1:
             l0.relax(vn, va, c_all, SIDE, SIDE + own)
-            halves = [
-                send(
-                    vn.at[pl.ds(2 + z_len, halo - 1)], vn.at[pl.ds(2, halo - 1)],
-                    v_send.at[0], v_recv.at[0], (zs[1], ys[0]),
-                ),
-                send(
-                    vn.at[pl.ds(1 + halo, halo - 1)],
-                    vn.at[pl.ds(1 + halo + z_len, halo - 1)],
-                    v_send.at[1], v_recv.at[1], (zs[gz - 1], ys[0]),
-                ),
-            ]
-            for copy in halves:
+            y_half = conc.shape[1] * gy // 2
+            half = pl.ds(pl.multiple_of(core * y_half, y_half), y_half)
+            sides = []
+            for n, (dz, start, to) in enumerate(
+                ((1, 2 + z_len, 2), (gz - 1, 1 + halo, 1 + halo + z_len))
+            ):
+                came = vn.at[pl.ds(to, halo - 1), half]
+                sides.append((n, came, send(
+                    vn.at[pl.ds(start, halo - 1), half], came,
+                    v_send.at[n], v_recv.at[n], (zs[dz], ys[0]),
+                )))
+            relays = []
+            for n, came, copy in sides:
+                copy.wait_recv()
+                relays.append(send(
+                    came, came, v_send.at[2 + n], v_recv.at[2 + n], (zs[0], sibling)
+                ))
+            for copy in relays:
                 copy.wait_recv()
         else:
             l0.relax(vb, va, c_all, SIDE, SIDE + own)
@@ -408,6 +444,7 @@
     nz2 = z_len // BLOCK * gz
     z_all = blocks * BLOCK
     near = 3 * gy - 1
+    assert z_len // BLOCK == BLOCK and gy % 2 == 0
 
     def vmem(*shape):
         return pltpu.VMEM(shape + (x_len,), jnp.float32)
@@ -420,15 +457,16 @@
         vmem(z_all + 2, y_all), vmem(z_all + 2, y_all), vmem(z_all + 2, y_all),
         vmem(z_all // 2, y_all), vmem(z_all // 2 + 2, y_all), vmem(z_all // 2 + 2, y_all),
         vmem(z_len // BLOCK, y_all), vmem(blocks + 2, y_all),
-        vmem(nz2 + 2, y2), vmem(CYCLES, nz2, y2), vmem(nz2 + 2, y2), vmem(nz2 + 2, y2),
+        vmem(nz2 + 2, y2), vmem(nz2, y2), vmem(nz2 + 2, y2), vmem(nz2 + 2, y2),
     ]
     for rows in (nz2 // 2, nz2 // 4):
         scratch += [vmem(rows + 2, y2), vmem(rows, y2), vmem(rows + 2, y2), vmem(rows + 2, y2)]
     scratch += [vmem(10, blocks, y_all), vmem(10, blocks, y_all)]
     scratch += [vmem(8, rows, y2) for rows in (nz2, nz2 // 2, nz2 // 4)]
-    scratch += [sems(near)] * 4 + [sems(gz - 1)] * 2 + [sems(CYCLES, gz - 1)] * 2 + [sems(2)] * 2
+    scratch += [sems(near)] * 4 + [sems(gz - 1)] * 2 + [sems(CYCLES, gz - 1)] * 2 + [sems(4)] * 2
     planes = (z_len // BLOCK, y_len, x_len)
     scratch += [sems(1 + 2 * planes[0])] + [pltpu.VMEM(planes, jnp.int32)] * 2
+    scratch += [vmem(gz, y2), vmem(CYCLES, gz, y2)]
     in_hbm = pl.BlockSpec(memory_space=pl.ANY)
     in_vmem = pl.BlockSpec(memory_space=pltpu.VMEM)
     in_smem = pl.BlockSpec(memory_space=pltpu.SMEM)

time: 57.7 us -> 50.6 us (0.88)
  Pallas kernels: 56 us -> 48.9 us
    pallas_call x1, Pallas kernels: 56 us -> 48.9 us  [per_device(): pl.pallas_call(functools.partial(kernel, gz, gy), out_shape=jax.ShapeDtyp...]
where the time goes in v3:
time: 50.6 us; the launch traced here: 50.4 us
  Pallas kernels  48.9 us (97%)
  local copies, waits for them, and re-layouts  1.47 us (3%)
    pallas_call x1, Pallas kernels, per_device(): pl.pallas_call(functools.partial(kernel, gz, gy), out_shape=jax.ShapeDtyp...  48.9 us
    unnamed x1, local copies, waits for them, and re-layouts  1.47 us

profile of v3, /device:TPU:0, one launch (start us, length us, event | category | flops | bytes accessed | tf_op | source)
XLA Modules:
  0.0 50.4 jit_solution(7345492626622959648)
XLA Ops:
  0.0 48.9 %shard_map.55 = f32[16,8,128]{2,1,0:T(8,128)} custom-call(f32[16,8,128]{2,1,0:T(8,128)} %conc.1, s32[16,8,128]{2,1,0:T(8,128)} %phases.1, s32[16,8,128]{2,1,0:T(8,128)} %grains.1, s32[64]{0:T(128)} %grain_class.1, f32[3,4]{1,0:T(4,128)} %diffusivity.1), custom_call_target="tpu_custom_call" | custom-call | tf_op jit(solution)/shard_map/pallas_call | solution.py:473
  48.9 1.5 %copy.7 = f32[16,8,128]{2,1,0:T(8,128)} copy(f32[16,8,128]{2,1,0:T(8,128)} %shard_map.55) | data formatting | bytes 131072
